TPU v7x, 256 devices: a whole 4x4x8 slice. The times are simulated.
256 devices in a mesh: rep: 8 (over x, core), exp: 32 (over y, z).
Axes of the slice: x: 4, y: 4, z: 8, core: 2. Of those that a mesh axis runs over, the one named last changes fastest.
Arguments:
- latent: float32 [32768, 2048], P(('rep', 'exp')), may hold values from -6 to 6
- targets: bfloat16 [1, 32768, 2048], P(None, ('rep', 'exp')), may hold values from -6 to 6
- norm_gain: float32 [2048], replicated, may hold values from 0.25 to 1.75
- router: bfloat16 [2048, 32], replicated, may hold values from -0.125 to 0.125
- expert_ids: int32 [1, 32768, 6], P(None, ('rep', 'exp')), may hold values from 0 to 31, all different within a row; in each aligned block of 128 rows (0 to 127, 128 to 255, ..., all dimensions but the last counted through in order) at most 25 rows name the same one
- gate_valid: int32 [1, 32768, 6], P(None, ('rep', 'exp')), may hold values 0 or 1
- w_gate: bfloat16 [32, 2048, 704], P('exp', 'rep'), may hold values from -0.125 to 0.125
- w_up: bfloat16 [32, 2048, 704], P('exp', 'rep'), may hold values from -0.125 to 0.125
- w_down: bfloat16 [32, 704, 2048], P('exp', None, 'rep'), may hold values from -0.21875 to 0.21875
Outputs:
- grad_latent: float32 [32768, 2048], P(('rep', 'exp'))
- grad_router: float32 [2048, 32], replicated
- grad_gain: float32 [2048], replicated
Inputs may be any that keep to these rules, and one draw needn't show every extreme that they name: `expert_ids`: within the 128 tokens of one device at one step, the 6 picks of a token differ, no expert is named more than 25 times, a bound that some block reaches.
All inputs are finite; a program needn't handle non-finite values. No bound on the sum of `gate_valid` on one device may be relied on, other than what follows from the above.
Results may differ from a plain program's by a relative error of at most 0.0051.
Values may be sent and summed in bfloat16 or wider, within the bound.
No kernel may reach another device: no remote copies, remote signals or barrier semaphores. Data moves between devices by JAX's collectives and lax.ppermute only.
A program may use at most 128 MiB of HBM per device.

v0:
```python
import jax
import jax.numpy as jnp
from jax import lax
from jax.sharding import PartitionSpec as P

UNROLL = 1
epsilon = 1e-06
highest = lax.Precision.HIGHEST


def norm_rows(latent, norm_gain):
    inv_scale = lax.rsqrt(jnp.mean(latent * latent, axis=-1, keepdims=True) + epsilon)
    return (inv_scale, (latent * inv_scale * norm_gain).astype(jnp.bfloat16))


def contract_first(left, right, precision=None):
    return lax.dot_general(
        left,
        right,
        (((0,), (0,)), ((), ())),
        precision=precision,
        preferred_element_type=jnp.float32,
    )


def contract_last(left, right, precision=None):
    return lax.dot_general(
        left,
        right,
        (((1,), (1,)), ((), ())),
        precision=precision,
        preferred_element_type=jnp.float32,
    )


def dispatch_tables(chosen_ids, expert_count, capacity):
    tok_rows, top_count = chosen_ids.shape
    flat_ids = chosen_ids.reshape(-1)
    experts_row = jnp.arange(expert_count, dtype=jnp.int32)
    onehot = (flat_ids[:, None] == experts_row[None, :]).astype(jnp.int32)
    before = jnp.cumsum(onehot, axis=0) - onehot
    slot_index = jnp.sum(before * onehot, axis=1)
    target_slot = flat_ids * capacity + slot_index
    slot_row = jnp.arange(expert_count * capacity, dtype=jnp.int32)
    spread = jnp.sum(
        (target_slot.reshape(tok_rows, top_count)[:, :, None] == slot_row[None, None, :]).astype(
            jnp.float32
        ),
        axis=1,
    ).astype(jnp.bfloat16)
    onehot_ids = (chosen_ids[:, :, None] == experts_row[None, None, :]).astype(jnp.float32)
    return (spread, onehot_ids, target_slot)


def shards(latent, targets, norm_gain, router, expert_ids, gate_valid, w_gate, w_up, w_down):
    tok_rows, features = latent.shape
    top_count = expert_ids.shape[2]
    expert_count = lax.axis_size("exp")
    capacity = tok_rows * top_count // expert_count + 1
    slot_count = expert_count * capacity
    gate_full, up_full = (
        lax.all_gather(w_gate, "rep", axis=1, tiled=True),
        lax.all_gather(w_up, "rep", axis=1, tiled=True),
    )
    down_full = lax.all_gather(w_down, "rep", axis=2, tiled=True)
    gate_weight, up_weight, down_weight = (gate_full[0], up_full[0], down_full[0])
    hidden_width = gate_weight.shape[1]
    latent_now = latent
    unroll = 0
    chosen_ids = expert_ids[unroll]
    validity = gate_valid[unroll].astype(jnp.float32)
    inv_scale, normed = norm_rows(latent_now, norm_gain)
    logits = jnp.dot(normed, router, preferred_element_type=jnp.float32)
    spread, onehot_ids, target_slot = dispatch_tables(chosen_ids, expert_count, capacity)
    picked = jnp.einsum("te,tke->tk", logits, onehot_ids, precision=highest)
    sigmoid_pick = jax.nn.sigmoid(picked)
    gating = sigmoid_pick * validity
    outgoing = (
        contract_first(spread, normed)
        .astype(jnp.bfloat16)
        .reshape(expert_count, capacity, features)
    )
    received = lax.all_to_all(outgoing, "exp", split_axis=0, concat_axis=0, tiled=True)
    row_block = received.reshape(-1, features)
    expert_hidden_gate = jnp.dot(row_block, gate_weight, preferred_element_type=jnp.float32)
    expert_hidden_up = jnp.dot(row_block, up_weight, preferred_element_type=jnp.float32)
    activated = (jax.nn.silu(expert_hidden_gate) * expert_hidden_up).astype(jnp.bfloat16)
    expert_out = jnp.dot(activated, down_weight, preferred_element_type=jnp.float32).astype(
        jnp.bfloat16
    )
    returned = lax.all_to_all(
        expert_out.reshape(received.shape), "exp", split_axis=0, concat_axis=0, tiled=True
    )
    stacked = (received.shape[0], received.shape[1], hidden_width)
    result = (
        returned,
        received,
        expert_hidden_gate.reshape(stacked),
        expert_hidden_up.reshape(stacked),
    )
    returned = result[0].reshape(slot_count, features)
    picked_rows = jnp.take(returned, target_slot, axis=0).reshape(tok_rows, top_count, features)
    mixed = jnp.sum(gating[:, :, None] * picked_rows.astype(jnp.float32), axis=1)
    saved = [
        (
            latent_now,
            inv_scale,
            normed,
            sigmoid_pick,
            validity,
            onehot_ids,
            spread,
            target_slot,
            gating,
            picked_rows,
            result[1:],
        )
    ]
    latent_now = latent_now + mixed
    cotangent = latent_now - targets[UNROLL - 1].astype(jnp.float32)
    router_grad = jnp.zeros((features, expert_count), jnp.float32)
    gain_grad = jnp.zeros((features,), jnp.float32)
    for unroll in reversed(range(UNROLL)):
        (
            earlier,
            inv_scale,
            normed,
            sigmoid_pick,
            validity,
            onehot_ids,
            spread,
            target_slot,
            gating,
            picked_rows,
            kept,
        ) = saved[unroll]
        hidden_gate = kept[1].reshape(slot_count, hidden_width)
        hidden_up = kept[2].reshape(slot_count, hidden_width)
        grad_gating = jnp.sum(cotangent[:, None, :] * picked_rows.astype(jnp.float32), axis=2)
        grad_out = (gating[:, :, None] * cotangent[:, None, :]).astype(jnp.bfloat16)
        outgoing = (
            jnp.zeros((slot_count, features), jnp.bfloat16)
            .at[target_slot]
            .set(grad_out.reshape(-1, features))
        )
        grad_in = lax.all_to_all(
            outgoing.reshape(expert_count, capacity, features),
            "exp",
            split_axis=0,
            concat_axis=0,
            tiled=True,
        ).reshape(slot_count, features)
        grad_act = contract_last(grad_in, down_weight).astype(jnp.bfloat16)
        sigmoid_gate = jax.nn.sigmoid(hidden_gate)
        act_grad = grad_act.astype(jnp.float32)
        grad_hidden_gate = (
            act_grad * hidden_up * sigmoid_gate * (1.0 + hidden_gate * (1.0 - sigmoid_gate))
        ).astype(jnp.bfloat16)
        grad_hidden_up = (act_grad * jax.nn.silu(hidden_gate)).astype(jnp.bfloat16)
        grad_rows = (
            contract_last(grad_hidden_gate, gate_weight) + contract_last(grad_hidden_up, up_weight)
        ).astype(jnp.bfloat16)
        grad_back = lax.all_to_all(
            grad_rows.reshape(expert_count, capacity, features),
            "exp",
            split_axis=0,
            concat_axis=0,
            tiled=True,
        ).reshape(slot_count, features)
        grad_normed = jnp.dot(spread, grad_back, preferred_element_type=jnp.float32)
        grad_pick = grad_gating * validity * sigmoid_pick * (1.0 - sigmoid_pick)
        grad_logits = jnp.einsum("tk,tke->te", grad_pick, onehot_ids, precision=highest).astype(
            jnp.bfloat16
        )
        router_grad = contract_first(normed, grad_logits)
        grad_normed = grad_normed + contract_last(grad_logits, router)
        gain_grad = jnp.sum(grad_normed * earlier * inv_scale, axis=0)
        scaled = grad_normed * norm_gain
        cube = inv_scale * inv_scale * inv_scale
        cotangent = (
            cotangent
            + inv_scale * scaled
            - earlier * cube * jnp.mean(scaled * earlier, axis=-1, keepdims=True)
        )
    grad_router, grad_gain = lax.psum((router_grad, gain_grad), ("rep", "exp"))
    return (cotangent, grad_router, grad_gain)


def solution(mesh):
    return jax.shard_map(
        shards,
        mesh=mesh,
        in_specs=(
            P(("rep", "exp"), None),
            P(None, ("rep", "exp"), None),
            P(),
            P(),
            P(None, ("rep", "exp"), None),
            P(None, ("rep", "exp"), None),
            P("exp", "rep", None),
            P("exp", "rep", None),
            P("exp", None, "rep"),
        ),
        out_specs=(P(("rep", "exp"), None), P(), P()),
        check_vma=False,
    )
```

profile of v0, /device:TPU:2, one launch (start us, length us, event | category | flops | bytes accessed | tf_op | source)
XLA Modules:
  0.0 714.2 jit_solution(9169743806705154316)
XLA Ops:
  19.4 11.6 %all-to-all-start = ((bf16[32,25,2048]{2,1,0:T(8,128)(2,1)}), bf16[32,25,2048]{2,1,0:T(8,128)(2,1)}, u32[]{:S(2)}, u32[]{:S(2)}) async-start(bf16[32,25,2048]{2,1,0:T(8,128)(2,1)} %reshape.145), calls=%async_computation | async-start | bytes 8388608 | tf_op jit(solution)/shard_map/all_to_all | solution.py:83
  31.8 96.5 %all-to-all-done = bf16[32,25,2048]{2,1,0:T(8,128)(2,1)} async-done(((bf16[32,25,2048]{2,1,0:T(8,128)(2,1)}), bf16[32,25,2048]{2,1,0:T(8,128)(2,1)}, u32[]{:S(2)}, u32[]{:S(2)}) %all-to-all-start) | async-done | bytes 3276832 | tf_op jit(solution)/shard_map/all_to_all | solution.py:83
  128.2 3.4 reshape.146
  131.7 6.0 fusion.10
  137.7 6.0 fusion.6
  143.7 6.0 convolution_convert_fusion
  152.7 5.4 all-to-all-start.1
  160.8 94.0 %all-to-all-done.1 = bf16[32,25,2048]{2,1,0:T(8,128)(2,1)} async-done(((bf16[32,25,2048]{2,1,0:T(8,128)(2,1)}), bf16[32,25,2048]{2,1,0:T(8,128)(2,1)}, u32[]{:S(2)}, u32[]{:S(2)}) %all-to-all-start.1) | async-done | bytes 3276832 | tf_op jit(solution)/shard_map/all_to_all | solution.py:91
  254.8 3.4 reshape.148
  258.2 4.4 gather_fusion
  262.6 6.3 gather.7
  268.9 6.1 multiply_reduce_fusion
  276.2 4.3 mul.195
  280.5 8.2 %mul.196 = f32[768,2048]{1,0:T(8,128)} reshape(f32[128,6,2048]{2,1,0:T(8,128)} %mul.195) | data formatting | bytes 12582912 | tf_op jit(solution)/shard_map/mul | solution.py:140
  288.7 9.7 %scatter_custom_fusion = bf16[800,2048]{1,0:T(8,128)(2,1)S(1)} fusion(s32[768]{0:T(1024)} %copy-done.19, f32[768,2048]{1,0:T(8,128)} %mul.196, f32[768]{0:T(1024)} %mul.193, bf16[]{:T(256)} %constant.40.clone.1), kind=kCustom, calls=%fused_computation.8 | custom fusion | flops 3145728 | bytes 9572864 | tf_op jit(solution)/shard_map/scatter | solution.py:144
  301.3 101.4 %all_to_all.20 = bf16[32,25,2048]{2,1,0:T(8,128)(2,1)} all-to-all(bf16[32,25,2048]{2,1,0:T(8,128)(2,1)} %reshape.149), channel_id=1, replica_groups=mesh['rep'=8,'exp'=32] {'exp'}, dimensions={0} | all-to-all | bytes 6553600 | tf_op jit(solution)/shard_map/all_to_all | solution.py:146
  402.7 3.4 reshape.150
  406.1 4.7 fusion.18
  420.0 5.3 all-to-all-start.3
  425.6 3.8 multiply_reduce_fusion.1
  432.2 90.3 %all-to-all-done.3 = bf16[32,25,2048]{2,1,0:T(8,128)(2,1)} async-done(((bf16[32,25,2048]{2,1,0:T(8,128)(2,1)}), bf16[32,25,2048]{2,1,0:T(8,128)(2,1)}, u32[]{:S(2)}, u32[]{:S(2)}) %all-to-all-start.3) | async-done | bytes 3276832 | tf_op jit(solution)/shard_map/all_to_all | solution.py:163
  522.5 3.4 reshape.152
  529.8 73.4 %psum.15 = f32[2048]{0:T(1024)} all-reduce(f32[2048]{0:T(1024)S(1)} %get-tuple-element.3), channel_id=1, replica_groups=mesh['rep'=8,'exp'=32] {'rep','exp'}, use_global_device_ids=true, to_apply=%region_11.12 | all-reduce | flops 2048 | bytes 16384 | tf_op jit(solution)/shard_map/psum | solution.py:185
  603.1 102.9 %all-reduce.2.cloned.1.call-done = f32[2048,32]{0,1:T(8,128)} async-done(((f32[2048,32]{0,1:T(8,128)}), f32[2048,32]{0,1:T(8,128)}) %all-reduce.2.cloned.1.call-update) | async-done | bytes 262160 | tf_op jit(solution)/shard_map/psum | solution.py:185
  (112 shorter events, 39.9 us)
Async XLA Ops:
  7.2 151.3 %copy-start = (bf16[2048,32]{0,1:T(8,128)(2,1)S(1)}, bf16[2048,32]{0,1:T(8,128)(2,1)}, u32[]{:S(2)}) copy-start(bf16[2048,32]{0,1:T(8,128)(2,1)} %param.12) | copy-start | bytes 393220
  7.2 7.3 %copy-start.2 = (f32[128,2048]{1,0:T(8,128)S(1)}, f32[128,2048]{1,0:T(8,128)}, u32[]{:S(2)}) copy-start(f32[128,2048]{1,0:T(8,128)} %param.9) | copy-start | bytes 3145732
  7.2 7.3 %copy-start.15 = (f32[2048]{0:T(1024)S(1)}, f32[2048]{0:T(1024)}, u32[]{:S(2)}) copy-start(f32[2048]{0:T(1024)} %param.11) | copy-start | bytes 24580
  7.2 124.5 %all-gather.4.cloned.1.call-start = ((), (), s32[]{:S(2)}) async-start(), calls=%async_computation.4 | async-start | bytes 3244032 | tf_op jit(solution)/shard_map/all_gather | solution.py:62
  7.9 129.8 %all-gather.6.cloned.1.call-start = ((), (), s32[]{:S(2)}) async-start(), calls=%async_computation.5 | async-start | bytes 3244032 | tf_op jit(solution)/shard_map/all_gather | solution.py:63
  11.9 2.6 copy-start.17
  19.4 108.8 %all-to-all-start = ((bf16[32,25,2048]{2,1,0:T(8,128)(2,1)}), bf16[32,25,2048]{2,1,0:T(8,128)(2,1)}, u32[]{:S(2)}, u32[]{:S(2)}) async-start(bf16[32,25,2048]{2,1,0:T(8,128)(2,1)} %reshape.145), calls=%async_computation | async-start | bytes 8388608 | tf_op jit(solution)/shard_map/all_to_all | solution.py:83
  31.0 112.6 %all-gather.8.cloned.1.call-start = ((), (), s32[]{:S(2)}) async-start(), calls=%async_computation.6 | async-start | bytes 3244032 | tf_op jit(solution)/shard_map/all_gather | solution.py:65
  152.6 5.4 copy-start.20
  152.6 5.7 copy-start.23
  152.6 5.8 copy-start.8
  152.6 7.5 %copy-start.18 = (s32[768]{0:T(1024)S(1)}, s32[768]{0:T(1024)}, u32[]{:S(2)}) copy-start(s32[768]{0:T(1024)} %copy-done.17) | copy-start | bytes 9220
  152.7 102.2 %all-to-all-start.1 = ((bf16[32,25,2048]{2,1,0:T(8,128)(2,1)}), bf16[32,25,2048]{2,1,0:T(8,128)(2,1)}, u32[]{:S(2)}, u32[]{:S(2)}) async-start(bf16[32,25,2048]{2,1,0:T(8,128)(2,1)} %reshape.147), calls=%async_computation.1 | async-start | bytes 8388608 | tf_op jit(solution)/shard_map/all_to_all | solution.py:91
  262.6 6.3 copy-start.11
  268.9 6.1 copy-start.3
  268.9 6.1 copy-start.12
  406.1 4.7 copy-start.25
  406.1 4.7 copy-start.27
  406.1 4.7 copy-start.28
  410.9 3.1 copy-start.26
  420.0 5.6 copy-start.1
  420.0 102.5 %all-to-all-start.3 = ((bf16[32,25,2048]{2,1,0:T(8,128)(2,1)}), bf16[32,25,2048]{2,1,0:T(8,128)(2,1)}, u32[]{:S(2)}, u32[]{:S(2)}) async-start(bf16[32,25,2048]{2,1,0:T(8,128)(2,1)} %reshape.151), calls=%async_computation.3 | async-start | bytes 8388608 | tf_op jit(solution)/shard_map/all_to_all | solution.py:163
  425.4 280.6 %all-reduce.2.cloned.1.call-start = ((), (), s32[]{:S(2)}) async-start(), calls=%async_computation.7 | async-start | bytes 524288 | tf_op jit(solution)/shard_map/psum | solution.py:185
  425.6 3.9 copy-start.14
  (12 other events, 19.8 us)
Sparse Core Ops, SparseCore 0:
  9.9 35.5 all-gather.3
  47.3 34.0 all-gather.5
  83.3 34.0 all-gather.7
  432.3 273.6 all-reduce.1
where the time goes:
time: 715 us; the launch traced here: 714 us
  waiting for transfers between devices  386 us (54%)
  blocking collectives  175 us (24%)
  local copies, waits for them, and re-layouts  54.9 us (8%)
  matrix products  35.8 us (5%)
  other arithmetic  26.1 us (4%)
  starting transfers between devices  22.5 us (3%)
  between operations  14.3 us (2%)
    psum x1, waiting for transfers between devices, shards(): grad_router, grad_gain = lax.psum((router_grad, gain_grad), ('rep', 'exp'))  103 us
    all_to_all x1, blocking collectives, shards(): lax.all_to_all(outgoing.reshape(expert_count, capacity, features), 'exp',...  101 us
    all_to_all x1, waiting for transfers between devices, shards(): lax.all_to_all(outgoing, 'exp', split_axis=0, concat_axis=0, tiled=True)  96.5 us
    all_to_all x1, waiting for transfers between devices, shards(): lax.all_to_all(expert_out.reshape(received.shape), 'exp', split_axis=0, c...  94 us
    all_to_all x1, waiting for transfers between devices, shards(): lax.all_to_all(grad_rows.reshape(expert_count, capacity, features), 'exp'...  90.3 us
    psum x1, blocking collectives, shards(): grad_router, grad_gain = lax.psum((router_grad, gain_grad), ('rep', 'exp'))  73.4 us
  transfers between devices with their start and end apart: 7, of which 4 were waited for; matrix products, arithmetic and copies ran while one was open for 6% of the time, Pallas kernels for 0%

commit v1 on v0

--- a/solution.py
+++ b/solution.py
@@ -182,7 +182,7 @@
             + inv_scale * scaled
             - earlier * cube * jnp.mean(scaled * earlier, axis=-1, keepdims=True)
         )
-    grad_router, grad_gain = lax.psum((router_grad, gain_grad), ("rep", "exp"))
+    grad_router, grad_gain = lax.psum(lax.psum((router_grad, gain_grad), "rep"), "exp")
     return (cotangent, grad_router, grad_gain)
 
 

time: 715 us -> 657 us (0.919)
  waiting for transfers between devices: 386 us -> 317 us
  blocking collectives: 175 us -> 185 us
    all_to_all x1, waiting for transfers between devices: 90.3 us -> 24.3 us  [shards(): lax.all_to_all(grad_rows.reshape(expert_count, capacity, features), 'exp'...]
    psum x1 -> x2, blocking collectives: 73.4 us -> 83.6 us  [the longest x1 73 us: shards(): lax.psum(lax.psum((router_grad, gain_grad), 'rep'), 'exp')]
    psum x1 -> x2, waiting for transfers between devices: 103 us -> 100 us  [the longest x1 65.5 us: shards(): lax.psum((router_grad, gain_grad), 'rep')]
  transfers between devices with their start and end apart: 7 -> 8, of which waited for: 4 -> 5; matrix products, arithmetic and copies ran while one was open for 6% -> 6% of each run, Pallas kernels for 0% -> 0%
where the time goes in v1:
time: 657 us; the launch traced here: 656 us
  waiting for transfers between devices  317 us (48%)
  blocking collectives  185 us (28%)
  local copies, waits for them, and re-layouts  55 us (8%)
  matrix products  35.8 us (5%)
  other arithmetic  26.1 us (4%)
  starting transfers between devices  22.6 us (3%)
  between operations  14.4 us (2%)
    all_to_all x1, blocking collectives, shards(): lax.all_to_all(outgoing.reshape(expert_count, capacity, features), 'exp',...  101 us
    all_to_all x1, waiting for transfers between devices, shards(): lax.all_to_all(outgoing, 'exp', split_axis=0, concat_axis=0, tiled=True)  96.5 us
    all_to_all x1, waiting for transfers between devices, shards(): lax.all_to_all(expert_out.reshape(received.shape), 'exp', split_axis=0, c...  94 us
    psum x1, blocking collectives, shards(): lax.psum(lax.psum((router_grad, gain_grad), 'rep'), 'exp')  73 us
    psum x1, waiting for transfers between devices, shards(): lax.psum((router_grad, gain_grad), 'rep')  65.5 us
    psum x1, waiting for transfers between devices, shards(): lax.psum(lax.psum((router_grad, gain_grad), 'rep'), 'exp')  34.7 us
    all_to_all x1, waiting for transfers between devices, shards(): lax.all_to_all(grad_rows.reshape(expert_count, capacity, features), 'exp'...  24.3 us
  transfers between devices with their start and end apart: 8, of which 5 were waited for; matrix products, arithmetic and copies ran while one was open for 6% of the time, Pallas kernels for 0%

profile of v1, /device:TPU:2, one launch (start us, length us, event | category | flops | bytes accessed | tf_op | source)
XLA Modules:
  0.0 655.8 jit_solution(12448759436384098087)
XLA Ops:
  19.4 11.6 %all-to-all-start = ((bf16[32,25,2048]{2,1,0:T(8,128)(2,1)}), bf16[32,25,2048]{2,1,0:T(8,128)(2,1)}, u32[]{:S(2)}, u32[]{:S(2)}) async-start(bf16[32,25,2048]{2,1,0:T(8,128)(2,1)} %reshape.145), calls=%async_computation | async-start | bytes 8388608 | tf_op jit(solution)/shard_map/all_to_all | solution.py:83
  31.8 96.5 %all-to-all-done = bf16[32,25,2048]{2,1,0:T(8,128)(2,1)} async-done(((bf16[32,25,2048]{2,1,0:T(8,128)(2,1)}), bf16[32,25,2048]{2,1,0:T(8,128)(2,1)}, u32[]{:S(2)}, u32[]{:S(2)}) %all-to-all-start) | async-done | bytes 3276832 | tf_op jit(solution)/shard_map/all_to_all | solution.py:83
  128.2 3.4 reshape.146
  131.7 6.0 fusion.10
  137.7 6.0 fusion.6
  143.7 6.0 convolution_convert_fusion
  152.6 5.4 all-to-all-start.1
  160.8 94.0 %all-to-all-done.1 = bf16[32,25,2048]{2,1,0:T(8,128)(2,1)} async-done(((bf16[32,25,2048]{2,1,0:T(8,128)(2,1)}), bf16[32,25,2048]{2,1,0:T(8,128)(2,1)}, u32[]{:S(2)}, u32[]{:S(2)}) %all-to-all-start.1) | async-done | bytes 3276832 | tf_op jit(solution)/shard_map/all_to_all | solution.py:91
  258.2 4.4 gather_fusion
  262.7 6.3 gather.7
  268.9 6.1 multiply_reduce_fusion
  276.2 4.3 mul.195
  280.5 8.2 %mul.196 = f32[768,2048]{1,0:T(8,128)} reshape(f32[128,6,2048]{2,1,0:T(8,128)} %mul.195) | data formatting | bytes 12582912 | tf_op jit(solution)/shard_map/mul | solution.py:140
  288.7 9.7 %scatter_custom_fusion = bf16[800,2048]{1,0:T(8,128)(2,1)S(1)} fusion(s32[768]{0:T(1024)} %copy-done.19, f32[768,2048]{1,0:T(8,128)} %mul.196, f32[768]{0:T(1024)} %mul.193, bf16[]{:T(256)} %constant.40.clone.1), kind=kCustom, calls=%fused_computation.8 | custom fusion | flops 3145728 | bytes 9572864 | tf_op jit(solution)/shard_map/scatter | solution.py:144
  301.3 101.4 %all_to_all.20 = bf16[32,25,2048]{2,1,0:T(8,128)(2,1)} all-to-all(bf16[32,25,2048]{2,1,0:T(8,128)(2,1)} %reshape.149), channel_id=1, replica_groups=mesh['rep'=8,'exp'=32] {'exp'}, dimensions={0} | all-to-all | bytes 6553600 | tf_op jit(solution)/shard_map/all_to_all | solution.py:146
  406.2 4.7 fusion.18
  420.1 5.3 all-to-all-start.3
  425.6 3.8 multiply_reduce_fusion.1
  432.3 65.5 %all-reduce.3.cloned.1.call-done = f32[2048,32]{0,1:T(8,128)} async-done(((f32[2048,32]{0,1:T(8,128)}), f32[2048,32]{0,1:T(8,128)}) %all-reduce.3.cloned.1.call-update) | async-done | bytes 262160 | tf_op jit(solution)/shard_map/psum | solution.py:185
  497.8 24.3 %all-to-all-done.3 = bf16[32,25,2048]{2,1,0:T(8,128)(2,1)} async-done(((bf16[32,25,2048]{2,1,0:T(8,128)(2,1)}), bf16[32,25,2048]{2,1,0:T(8,128)(2,1)}, u32[]{:S(2)}, u32[]{:S(2)}) %all-to-all-start.3) | async-done | bytes 3276832 | tf_op jit(solution)/shard_map/all_to_all | solution.py:163
  522.1 3.4 reshape.152
  529.3 10.6 %psum.30 = f32[2048]{0:T(1024)S(1)} all-reduce(f32[2048]{0:T(1024)S(1)} %get-tuple-element.3), channel_id=1, replica_groups=mesh['rep'=8,'exp'=32] {'rep'}, use_global_device_ids=true, to_apply=%region_12.13 | all-reduce | flops 2048 | bytes 16384 | tf_op jit(solution)/shard_map/psum | solution.py:185
  539.9 73.0 %psum.31 = f32[2048]{0:T(1024)} all-reduce(f32[2048]{0:T(1024)S(1)} %psum.30), channel_id=1, replica_groups=mesh['rep'=8,'exp'=32] {'exp'}, use_global_device_ids=true, to_apply=%region_13.14 | all-reduce | flops 2048 | bytes 16384 | tf_op jit(solution)/shard_map/psum | solution.py:185
  612.9 34.7 %all-reduce.5.cloned.1.call-done = f32[2048,32]{0,1:T(8,128)} async-done(((f32[2048,32]{0,1:T(8,128)}), f32[2048,32]{0,1:T(8,128)}) %all-reduce.5.cloned.1.call-update) | async-done | bytes 262160 | tf_op jit(solution)/shard_map/psum | solution.py:185
  (116 shorter events, 46.9 us)
Async XLA Ops:
  7.2 151.3 %copy-start = (bf16[2048,32]{0,1:T(8,128)(2,1)S(1)}, bf16[2048,32]{0,1:T(8,128)(2,1)}, u32[]{:S(2)}) copy-start(bf16[2048,32]{0,1:T(8,128)(2,1)} %param.12) | copy-start | bytes 393220
  7.2 7.3 %copy-start.2 = (f32[128,2048]{1,0:T(8,128)S(1)}, f32[128,2048]{1,0:T(8,128)}, u32[]{:S(2)}) copy-start(f32[128,2048]{1,0:T(8,128)} %param.9) | copy-start | bytes 3145732
  7.2 7.3 %copy-start.15 = (f32[2048]{0:T(1024)S(1)}, f32[2048]{0:T(1024)}, u32[]{:S(2)}) copy-start(f32[2048]{0:T(1024)} %param.11) | copy-start | bytes 24580
  7.2 124.5 %all-gather.4.cloned.1.call-start = ((), (), s32[]{:S(2)}) async-start(), calls=%async_computation.4 | async-start | bytes 3244032 | tf_op jit(solution)/shard_map/all_gather | solution.py:62
  7.9 129.8 %all-gather.6.cloned.1.call-start = ((), (), s32[]{:S(2)}) async-start(), calls=%async_computation.5 | async-start | bytes 3244032 | tf_op jit(solution)/shard_map/all_gather | solution.py:63
  19.4 108.8 %all-to-all-start = ((bf16[32,25,2048]{2,1,0:T(8,128)(2,1)}), bf16[32,25,2048]{2,1,0:T(8,128)(2,1)}, u32[]{:S(2)}, u32[]{:S(2)}) async-start(bf16[32,25,2048]{2,1,0:T(8,128)(2,1)} %reshape.145), calls=%async_computation | async-start | bytes 8388608 | tf_op jit(solution)/shard_map/all_to_all | solution.py:83
  31.0 112.7 %all-gather.8.cloned.1.call-start = ((), (), s32[]{:S(2)}) async-start(), calls=%async_computation.6 | async-start | bytes 3244032 | tf_op jit(solution)/shard_map/all_gather | solution.py:65
  152.6 5.4 copy-start.20
  152.6 5.7 copy-start.23
  152.6 5.8 copy-start.8
  152.6 7.5 %copy-start.18 = (s32[768]{0:T(1024)S(1)}, s32[768]{0:T(1024)}, u32[]{:S(2)}) copy-start(s32[768]{0:T(1024)} %copy-done.17) | copy-start | bytes 9220
  152.6 102.2 %all-to-all-start.1 = ((bf16[32,25,2048]{2,1,0:T(8,128)(2,1)}), bf16[32,25,2048]{2,1,0:T(8,128)(2,1)}, u32[]{:S(2)}, u32[]{:S(2)}) async-start(bf16[32,25,2048]{2,1,0:T(8,128)(2,1)} %reshape.147), calls=%async_computation.1 | async-start | bytes 8388608 | tf_op jit(solution)/shard_map/all_to_all | solution.py:91
  262.7 6.3 copy-start.11
  268.9 6.1 copy-start.3
  268.9 6.1 copy-start.12
  406.2 4.7 copy-start.25
  406.2 4.7 copy-start.27
  406.2 4.7 copy-start.28
  411.0 3.1 copy-start.26
  420.1 5.5 copy-start.1
  420.1 102.0 %all-to-all-start.3 = ((bf16[32,25,2048]{2,1,0:T(8,128)(2,1)}), bf16[32,25,2048]{2,1,0:T(8,128)(2,1)}, u32[]{:S(2)}, u32[]{:S(2)}) async-start(bf16[32,25,2048]{2,1,0:T(8,128)(2,1)} %reshape.151), calls=%async_computation.3 | async-start | bytes 8388608 | tf_op jit(solution)/shard_map/all_to_all | solution.py:163
  425.4 72.4 %all-reduce.3.cloned.1.call-start = ((), (), s32[]{:S(2)}) async-start(), calls=%async_computation.7 | async-start | bytes 524288 | tf_op jit(solution)/shard_map/psum | solution.py:185
  425.6 3.9 copy-start.14
  432.3 215.3 %all-reduce.5.cloned.1.call-start = ((), (), s32[]{:S(2)}) async-start(), calls=%async_computation.8 | async-start | bytes 524288 | tf_op jit(solution)/shard_map/psum | solution.py:185
  (13 other events, 22.4 us)
Sparse Core Ops, SparseCore 0:
  9.9 35.5 all-gather.3
  47.3 34.0 all-gather.5
  83.3 34.0 all-gather.7
  432.4 65.3 all-reduce.2
  501.5 146.0 all-reduce.4
